TPU v7x, 32 devices: a whole 2x2x4 slice. The times are simulated.
32 devices in a mesh: batch: 4 (over y, x), head: 8 (over z, core).
Axes of the slice: x: 2, y: 2, z: 4, core: 2. Of those that a mesh axis runs over, the one named last changes fastest.
Arguments:
- tokens: bfloat16 [8, 1024, 2048], P('batch', 'head'), may hold values from -6 to 6
- segment_ids: int32 [8, 1024], P('batch'), may hold values from 0 to 3, as said below
- position_ids: int32 [8, 1024], P('batch'), may hold values from 0 to 1023, as said below
- w_query: bfloat16 [2048, 2048], P('batch', 'head'), may hold values from -0.125 to 0.125
- w_key: bfloat16 [2048, 2048], P('batch', 'head'), may hold values from -0.125 to 0.125
- w_value: bfloat16 [2048, 2048], P('batch', 'head'), may hold values from -0.125 to 0.125
- w_output: bfloat16 [2048, 2048], P('batch', 'head'), may hold values from -0.75 to 0.75
- w_gate: bfloat16 [2048, 8192], P('batch', 'head'), may hold values from -0.125 to 0.125
- w_up: bfloat16 [2048, 8192], P('batch', 'head'), may hold values from -0.125 to 0.125
- w_down: bfloat16 [2048, 8192], P('batch', 'head'), may hold values from -0.0625 to 0.0625
- attn_gain: bfloat16 [2048], P('batch'), may hold values from 0.099609375 to 1.8984375
- mlp_gain: bfloat16 [2048], P('batch'), may hold values from 0.099609375 to 1.8984375
- cotangent: bfloat16 [8, 1024, 2048], P('batch', 'head'), may hold values from -6 to 6
Outputs:
- layer_out: bfloat16 [8, 1024, 2048], P('batch', 'head')
- grad_input: float32 [8, 1024, 2048], P('batch', 'head')
- grad_query: float32 [2048, 2048], P('batch', 'head')
- grad_key: float32 [2048, 2048], P('batch', 'head')
- grad_value: float32 [2048, 2048], P('batch', 'head')
- grad_output: float32 [2048, 2048], P('batch', 'head')
- grad_gate: float32 [2048, 8192], P('batch', 'head')
- grad_up: float32 [2048, 8192], P('batch', 'head')
- grad_down: float32 [2048, 8192], P('batch', 'head')
- grad_attn_gain: float32 [2048], P('batch')
- grad_mlp_gain: float32 [2048], P('batch')
Inputs may be any that keep to these rules, and one draw needn't show every extreme that they name: `segment_ids`: within a row the ids start at 0, rise by one at each document's first token and never fall. In every aligned block of 2 rows, one row (which one is drawn from the seed) is a single document of all 1024 tokens, and the next row in the block (cyclically) is cut into documents of exactly 256 tokens; in all other rows documents have 256 to 512 tokens except the last of a row, which may be shorter. `position_ids`: the token's index counted from its document's first token.
All inputs are finite; a program needn't handle non-finite values.
Results may differ from a plain program's by a relative error of at most 0.02.
Values may be sent and summed in bfloat16 or wider, within the bound.
A program may use at most 184 MiB of HBM per device.

v0:
```python
import jax
import jax.numpy as jnp
from jax import lax
from jax.sharding import PartitionSpec as P

HEAD_DIM = 64
epsilon = 1e-05
rope_base = 130000.0
masked_value = -1000000000.0


def normed(values, gain):
    inv_root = lax.rsqrt(jnp.mean(values * values, axis=-1, keepdims=True) + epsilon)
    return values * inv_root * gain


def norm_back(values, gain, grad):
    inv_root = lax.rsqrt(jnp.mean(values * values, axis=-1, keepdims=True) + epsilon)
    unit = values * inv_root
    weighted = grad * gain
    grad_values = inv_root * (weighted - unit * jnp.mean(weighted * unit, axis=-1, keepdims=True))
    return (grad_values, grad * unit)


def rope_tables(positions):
    half_dim = HEAD_DIM // 2
    frequency = rope_base ** (-(jnp.arange(half_dim).astype(jnp.float32) * 2.0) / HEAD_DIM)
    angles = positions.astype(jnp.float32)[:, None] * frequency[None, :]
    return (jnp.cos(angles)[:, None, :], jnp.sin(angles)[:, None, :])


def rotate(values, cosine, sine):
    half_dim = values.shape[-1] // 2
    first_half = values[..., :half_dim]
    second = values[..., half_dim:]
    return jnp.concatenate(
        [first_half * cosine - second * sine, second * cosine + first_half * sine], axis=-1
    )


def contract_rows(left, right):
    return lax.dot_general(
        left, right, (((0,), (0,)), ((), ())), preferred_element_type=jnp.float32
    )


def contract_cols(left, right):
    return lax.dot_general(
        left, right, (((1,), (1,)), ((), ())), preferred_element_type=jnp.float32
    )


def fetch_weights(w_query, w_key, w_value, w_output, w_gate, w_up, w_down, attn_gain, mlp_gain):
    return (
        lax.all_gather(w_query, "batch", axis=0, tiled=True),
        lax.all_gather(w_key, "batch", axis=0, tiled=True),
        lax.all_gather(w_value, "batch", axis=0, tiled=True),
        lax.all_gather(w_output, "batch", axis=0, tiled=True),
        lax.all_gather(w_gate, "batch", axis=0, tiled=True),
        lax.all_gather(w_up, "batch", axis=0, tiled=True),
        lax.all_gather(w_down, "batch", axis=0, tiled=True),
        lax.all_gather(attn_gain, "batch", axis=0, tiled=True),
        lax.all_gather(mlp_gain, "batch", axis=0, tiled=True),
    )


def reduce_grads(grad_parts):
    gain_sums = lax.psum((grad_parts[7], grad_parts[8]), "head")
    return (
        lax.psum_scatter(
            grad_parts[0].astype(jnp.bfloat16), "batch", scatter_dimension=0, tiled=True
        ).astype(jnp.float32),
        lax.psum_scatter(
            grad_parts[1].astype(jnp.bfloat16), "batch", scatter_dimension=0, tiled=True
        ).astype(jnp.float32),
        lax.psum_scatter(
            grad_parts[2].astype(jnp.bfloat16), "batch", scatter_dimension=0, tiled=True
        ).astype(jnp.float32),
        lax.psum_scatter(
            grad_parts[3].astype(jnp.bfloat16), "batch", scatter_dimension=0, tiled=True
        ).astype(jnp.float32),
        lax.psum_scatter(
            grad_parts[4].astype(jnp.bfloat16), "batch", scatter_dimension=0, tiled=True
        ).astype(jnp.float32),
        lax.psum_scatter(
            grad_parts[5].astype(jnp.bfloat16), "batch", scatter_dimension=0, tiled=True
        ).astype(jnp.float32),
        lax.psum_scatter(
            grad_parts[6].astype(jnp.bfloat16), "batch", scatter_dimension=0, tiled=True
        ).astype(jnp.float32),
        lax.psum_scatter(
            gain_sums[0].astype(jnp.bfloat16), "batch", scatter_dimension=0, tiled=True
        ).astype(jnp.float32),
        lax.psum_scatter(
            gain_sums[1].astype(jnp.bfloat16), "batch", scatter_dimension=0, tiled=True
        ).astype(jnp.float32),
    )


def block_scores(query, key_rot, segments, block_start):
    block_len = query.shape[0]
    scores = jnp.einsum(
        "qhd,khd->hqk", query, key_rot, preferred_element_type=jnp.float32
    ) * HEAD_DIM ** (-0.5)
    query_index = block_start + jnp.arange(block_len)[:, None]
    key_index = jnp.arange(key_rot.shape[0])[None, :]
    same_doc = segments[block_start : block_start + block_len][:, None] == segments[None, :]
    return (scores, (same_doc & (key_index <= query_index))[None, :, :])


def attend_forward(query, key_rot, values, segments):
    length = query.shape[0]
    block_len = min(512, length)
    results = []
    log_sums = []
    for block_start in range(0, length, block_len):
        scores, allowed = block_scores(
            query[block_start : block_start + block_len], key_rot, segments, block_start
        )
        masked = jnp.where(allowed, scores, masked_value)
        row_max = jnp.max(masked, axis=-1, keepdims=True)
        weights_exp = jnp.exp(masked - row_max)
        row_total = jnp.sum(weights_exp, axis=-1, keepdims=True)
        probabilities = (weights_exp / row_total).astype(jnp.bfloat16)
        results.append(
            jnp.einsum("hqk,khd->qhd", probabilities, values, preferred_element_type=jnp.float32)
        )
        log_sums.append(row_max + jnp.log(row_total))
    return (jnp.concatenate(results, axis=0), log_sums)


def attend_backward(query, key_rot, values, segments, log_sums, grad_out):
    length = query.shape[0]
    block_len = min(512, length)
    inv_scale = HEAD_DIM ** (-0.5)
    query_grads = []
    key_grad = jnp.zeros(key_rot.shape, jnp.float32)
    value_grad = jnp.zeros(values.shape, jnp.float32)
    for block_number, block_start in enumerate(range(0, length, block_len)):
        query_block = query[block_start : block_start + block_len]
        scores, allowed = block_scores(query_block, key_rot, segments, block_start)
        probs_full = jnp.exp(jnp.where(allowed, scores, masked_value) - log_sums[block_number])
        grad_block = grad_out[block_start : block_start + block_len]
        grad_prob = jnp.einsum(
            "qhd,khd->hqk", grad_block, values, preferred_element_type=jnp.float32
        )
        row_delta = jnp.sum(probs_full * grad_prob, axis=-1, keepdims=True)
        grad_score = (probs_full * (grad_prob - row_delta)).astype(jnp.bfloat16)
        query_grads.append(
            jnp.einsum("hqk,khd->qhd", grad_score, key_rot, preferred_element_type=jnp.float32)
            * inv_scale
        )
        key_grad = (
            key_grad
            + jnp.einsum(
                "hqk,qhd->khd", grad_score, query_block, preferred_element_type=jnp.float32
            )
            * inv_scale
        )
        value_grad = value_grad + jnp.einsum(
            "hqk,qhd->khd",
            probs_full.astype(jnp.bfloat16),
            grad_block,
            preferred_element_type=jnp.float32,
        )
    return (jnp.concatenate(query_grads, axis=0), key_grad, value_grad)


def per_device(
    tokens,
    segment_ids,
    position_ids,
    w_query,
    w_key,
    w_value,
    w_output,
    w_gate,
    w_up,
    w_down,
    attn_gain,
    mlp_gain,
    cotangent,
):
    row_count = tokens.shape[0]
    local_len = tokens.shape[1]
    offset = lax.axis_index("head") * local_len
    accumulated = None
    outputs = []
    input_grads = []
    for row_index in range(row_count):
        gathered = fetch_weights(
            w_query, w_key, w_value, w_output, w_gate, w_up, w_down, attn_gain, mlp_gain
        )
        query_w, key_w, value_w, output_w, gate_w, up_w, down_w = gathered[:7]
        gain_one = gathered[7].astype(jnp.float32)
        gain_two = gathered[8].astype(jnp.float32)
        segments = segment_ids[row_index]
        cosine, sine = rope_tables(position_ids[row_index])
        inputs = tokens[row_index].astype(jnp.float32)
        attn_in = lax.all_gather(
            normed(inputs, gain_one).astype(jnp.bfloat16), "head", axis=0, tiled=True
        )
        length = attn_in.shape[0]
        heads_here = query_w.shape[1] // HEAD_DIM
        head_shape = (length, heads_here, HEAD_DIM)
        query_lin = jnp.dot(attn_in, query_w, preferred_element_type=jnp.float32).reshape(
            head_shape
        )
        key_lin = jnp.dot(attn_in, key_w, preferred_element_type=jnp.float32).reshape(head_shape)
        query = rotate(query_lin, cosine, sine).astype(jnp.bfloat16)
        key_rot = rotate(key_lin, cosine, sine).astype(jnp.bfloat16)
        values = (
            jnp.dot(attn_in, value_w, preferred_element_type=jnp.float32)
            .astype(jnp.bfloat16)
            .reshape(head_shape)
        )
        attended, log_sums = attend_forward(query, key_rot, values, segments)
        attended = attended.reshape(length, heads_here * HEAD_DIM).astype(jnp.bfloat16)
        attn_terms = contract_cols(attended, output_w)
        token_rows = jnp.arange(length)
        own_rows = (token_rows >= offset) & (token_rows < offset + local_len)
        placed = lax.dynamic_update_slice_in_dim(jnp.zeros_like(attn_terms), inputs, offset, 0)
        mixed_full = lax.psum(attn_terms + placed, "head")
        mixed = lax.dynamic_slice_in_dim(mixed_full, offset, local_len, 0)
        mlp_in = normed(mixed_full, gain_two).astype(jnp.bfloat16)
        gate_act = jnp.dot(mlp_in, gate_w, preferred_element_type=jnp.float32)
        up_act = jnp.dot(mlp_in, up_w, preferred_element_type=jnp.float32)
        hidden = (jax.nn.silu(gate_act) * up_act).astype(jnp.bfloat16)
        mlp_terms = contract_cols(hidden, down_w)
        result = mixed + lax.psum_scatter(
            mlp_terms.astype(jnp.bfloat16), "head", scatter_dimension=0, tiled=True
        ).astype(jnp.float32)
        outputs.append(result.astype(jnp.bfloat16))
        grad_row = cotangent[row_index]
        grad_full = lax.all_gather(grad_row, "head", axis=0, tiled=True)
        grad_down = contract_rows(grad_full, hidden)
        grad_hidden = jnp.dot(grad_full, down_w, preferred_element_type=jnp.float32)
        _, pull_swish = jax.vjp(
            lambda gate_in, up_in: jax.nn.silu(gate_in) * up_in, gate_act, up_act
        )
        grad_gate_act, grad_up_act = pull_swish(grad_hidden)
        grad_gate_act = grad_gate_act.astype(jnp.bfloat16)
        grad_up_act = grad_up_act.astype(jnp.bfloat16)
        grad_gate = contract_rows(mlp_in, grad_gate_act)
        grad_up = contract_rows(mlp_in, grad_up_act)
        mlp_in_terms = contract_cols(grad_gate_act, gate_w) + contract_cols(grad_up_act, up_w)
        grad_mlp_in = lax.psum(mlp_in_terms, "head")
        grad_from_norm, gain_terms = norm_back(mixed_full, gain_two, grad_mlp_in)
        gain_two_grad = jnp.sum(jnp.where(own_rows[:, None], gain_terms, 0.0), axis=0)
        grad_mixed_full = grad_full.astype(jnp.float32) + grad_from_norm
        grad_mixed = lax.dynamic_slice_in_dim(grad_mixed_full, offset, local_len, 0)
        grad_att = grad_mixed_full.astype(jnp.bfloat16)
        grad_output = contract_rows(grad_att, attended)
        grad_attended = (
            jnp.dot(grad_att, output_w, preferred_element_type=jnp.float32)
            .astype(jnp.bfloat16)
            .reshape(head_shape)
        )
        query_rot_grad, key_rot_grad, value_rot_grad = attend_backward(
            query, key_rot, values, segments, log_sums, grad_attended
        )
        _, pull_rope = jax.vjp(
            lambda query_in, key_in: (rotate(query_in, cosine, sine), rotate(key_in, cosine, sine)),
            query_lin,
            key_lin,
        )
        query_pre_grad, key_pre_grad = pull_rope((query_rot_grad, key_rot_grad))
        query_grad_b = query_pre_grad.reshape(length, heads_here * HEAD_DIM).astype(jnp.bfloat16)
        key_grad_b = key_pre_grad.reshape(length, heads_here * HEAD_DIM).astype(jnp.bfloat16)
        value_grad_b = value_rot_grad.reshape(length, heads_here * HEAD_DIM).astype(jnp.bfloat16)
        grad_query = contract_rows(attn_in, query_grad_b)
        grad_key = contract_rows(attn_in, key_grad_b)
        grad_value = contract_rows(attn_in, value_grad_b)
        attn_in_terms = (
            contract_cols(query_grad_b, query_w)
            + contract_cols(key_grad_b, key_w)
            + contract_cols(value_grad_b, value_w)
        )
        grad_attn_in = lax.psum_scatter(
            attn_in_terms.astype(jnp.bfloat16), "head", scatter_dimension=0, tiled=True
        ).astype(jnp.float32)
        grad_from_first, first_terms = norm_back(inputs, gain_one, grad_attn_in)
        input_grads.append(grad_mixed + grad_from_first)
        grad_parts = (
            grad_query,
            grad_key,
            grad_value,
            grad_output,
            grad_gate,
            grad_up,
            grad_down,
            jnp.sum(first_terms, axis=0),
            gain_two_grad,
        )
        if accumulated is None:
            accumulated = grad_parts
        else:
            accumulated = jax.tree.map(jnp.add, accumulated, grad_parts)
    reduced = reduce_grads(accumulated)
    return (
        jnp.stack(outputs),
        jnp.stack(input_grads),
        reduced[0],
        reduced[1],
        reduced[2],
        reduced[3],
        reduced[4],
        reduced[5],
        reduced[6],
        reduced[7],
        reduced[8],
    )


def solution(mesh):
    placed = (
        P("batch", "head", None),
        P("batch", None),
        P("batch", None),
        P("batch", "head"),
        P("batch", "head"),
        P("batch", "head"),
        P("batch", "head"),
        P("batch", "head"),
        P("batch", "head"),
        P("batch", "head"),
        P("batch"),
        P("batch"),
        P("batch", "head", None),
    )
    return jax.shard_map(
        per_device,
        mesh=mesh,
        in_specs=placed,
        out_specs=(
            P("batch", "head", None),
            P("batch", "head", None),
            P("batch", "head"),
            P("batch", "head"),
            P("batch", "head"),
            P("batch", "head"),
            P("batch", "head"),
            P("batch", "head"),
            P("batch", "head"),
            P("batch"),
            P("batch"),
        ),
        check_vma=False,
    )
```

profile of v0, /device:TPU:0, one launch (start us, length us, event | category | flops | bytes accessed | tf_op | source)
XLA Modules:
  0.0 1740.3 jit_solution(4648591317237889378)
XLA Ops:
  8.7 9.5 all-gather.2
  28.9 10.3 all-gather.22.cloned.1.call-done
  39.2 49.3 %all-gather.32.cloned.1.call-done = bf16[1024,2048]{1,0:T(8,128)(2,1)} async-done(((bf16[128,2048]{1,0:T(8,128)(2,1)}), bf16[1024,2048]{1,0:T(8,128)(2,1)}) %all-gather.32.cloned.1.call-update) | async-done | bytes 4194320 | tf_op jit(solution)/shard_map/all_gather | solution.py:200
  92.4 23.4 %all-gather.20.cloned.1.call-done = bf16[2048,256]{1,0:T(8,128)(2,1)} async-done(((bf16[512,256]{1,0:T(8,128)(2,1)}), bf16[2048,256]{1,0:T(8,128)(2,1)}) %all-gather.20.cloned.1.call-update) | async-done | bytes 1048592 | tf_op jit(solution)/shard_map/all_gather | solution.py:55
  115.8 3.8 fusion.149
  121.9 5.4 fusion.142
  129.6 14.5 all-gather.18.cloned.1.call-done
  144.2 3.9 convolution_convert_fusion.2
  154.4 13.6 fusion.101
  168.0 25.3 %all-gather.16.cloned.1.call-done = bf16[1024,2048]{1,0:T(8,128)(2,1)} async-done(((bf16[128,2048]{1,0:T(8,128)(2,1)}), bf16[1024,2048]{1,0:T(8,128)(2,1)}) %all-gather.16.cloned.1.call-update) | async-done | bytes 4194320 | tf_op jit(solution)/shard_map/all_gather | solution.py:200
  212.1 8.6 all-gather.24.cloned.1.call-done
  220.7 5.9 fusion.151
  226.6 4.7 fusion.146
  238.3 8.1 all-gather.3
  246.4 321.8 %all-reduce.19.cloned.1.call-done = (f32[1024,2048]{1,0:T(8,128)}, f32[1024,2048]{1,0:T(8,128)}) async-done(((f32[1024,2048]{1,0:T(8,128)}, f32[1024,2048]{1,0:T(8,128)}), (f32[1024,2048]{1,0:T(8,128)}, f32[1024,2048]{1,0:T(8,128)})) %all-reduce.19.cloned.1.call-update) | async-done | bytes 16777232 | tf_op jit(solution)/shard_map/psum | solution.py:223
  568.2 4.1 multiply_reduce_fusion.6
  576.6 4.6 multiply_convert_fusion.5
  581.2 41.7 %all-gather.28.cloned.1.call-done = bf16[2048,1024]{1,0:T(8,128)(2,1)} async-done(((bf16[512,1024]{1,0:T(8,128)(2,1)}), bf16[2048,1024]{1,0:T(8,128)(2,1)}) %all-gather.28.cloned.1.call-update) | async-done | bytes 4194320 | tf_op jit(solution)/shard_map/all_gather | solution.py:60
  622.9 9.9 fusion.153
  632.8 44.7 %all-gather.26.cloned.1.call-done = bf16[2048,1024]{1,0:T(8,128)(2,1)} async-done(((bf16[512,1024]{1,0:T(8,128)(2,1)}), bf16[2048,1024]{1,0:T(8,128)(2,1)}) %all-gather.26.cloned.1.call-update) | async-done | bytes 4194320 | tf_op jit(solution)/shard_map/all_gather | solution.py:59
  677.5 10.0 fusion.152
  687.5 44.4 %all-gather.30.cloned.1.call-done = bf16[2048,1024]{1,0:T(8,128)(2,1)} async-done(((bf16[512,1024]{1,0:T(8,128)(2,1)}), bf16[2048,1024]{1,0:T(8,128)(2,1)}) %all-gather.30.cloned.1.call-update) | async-done | bytes 4194320 | tf_op jit(solution)/shard_map/all_gather | solution.py:61
  731.9 49.4 %all-gather.36.cloned.1.call-done = bf16[1,1024,2048]{2,1,0:T(8,128)(2,1)} async-done(((bf16[1,128,2048]{2,1,0:T(8,128)(2,1)}), bf16[1,1024,2048]{2,1,0:T(8,128)(2,1)}) %all-gather.36.cloned.1.call-update) | async-done | bytes 4194320 | tf_op jit(solution)/shard_map/all_gather | solution.py:235
  781.3 13.2 multiply_convert_fusion.6
  794.5 6.9 fusion.157
  801.5 6.1 fusion.148
  807.6 6.1 fusion.147
  813.7 15.5 all-gather.34.cloned.1.call-done
  829.2 13.2 multiply_convert_fusion.7
  842.4 4.6 fusion.154
  847.1 9.0 convolution_add_fusion
  856.1 7.2 convolution_add_fusion.1
  863.4 6.7 fusion.23
  870.2 6.3 fusion.22
  876.5 7.2 fusion.164
  883.7 6.1 add_convert_fusion.1
  890.0 7.4 fusion.163
  897.4 6.2 add_convert_fusion.2
  903.7 9.4 convolution_convert_fusion.1
  913.9 8.4 convolution_convert_fusion
  922.4 273.4 %all-reduce.17.cloned.1.call-done = (f32[1024,2048]{1,0:T(8,128)}, f32[1024,2048]{1,0:T(8,128)}) async-done(((f32[1024,2048]{1,0:T(8,128)}, f32[1024,2048]{1,0:T(8,128)}), (f32[1024,2048]{1,0:T(8,128)}, f32[1024,2048]{1,0:T(8,128)})) %all-reduce.17.cloned.1.call-update) | async-done | bytes 16777232 | tf_op jit(solution)/shard_map/psum | solution.py:247
  1195.8 14.5 select_reduce_fusion.1
  1210.4 22.6 %multiply_add_fusion.1 = (f32[1024,2048]{1,0:T(8,128)}, f32[1024,2048]{1,0:T(8,128)}) fusion(f32[1024,2048]{1,0:T(8,128)} %get-tuple-element.50, f32[1024,2048]{1,0:T(8,128)} %get-tuple-element.52, bf16[1,1024,2048]{2,1,0:T(8,128)(2,1)} %all-gather.34.cloned.1.call-done, f32[1024]{0:T(1024)S(1)} %broadcast_multiply_fusion.1, f32[2048]{0:T(1024)S(1)} %bitcast.256, ...), kind=kLoop, calls=%fused_computation.21 | loop fusion | flops 29360128 | bytes 58744832 | tf_op jit(solution)/shard_map/add | solution.py:250
  1233.0 4.8 fusion.85
  1237.9 8.3 multiply_reduce_fusion.1
  1248.0 4.6 multiply_convert_fusion.1
  1256.0 4.4 multiply_reduce_fusion
  1260.4 6.8 multiply_convert_fusion
  1267.2 4.9 fusion.93
  1272.1 4.4 multiply_reduce_fusion.4
  1276.6 4.5 multiply_convert_fusion.3
  1297.2 6.6 multiply_reduce_fusion.3
  1303.9 7.1 multiply_convert_fusion.2
  1316.1 5.4 fusion.14
  1370.4 44.7 %reduce-scatter.12.cloned.1.call-done = bf16[128,2048]{1,0:T(8,128)(2,1)} async-done(((bf16[1024,2048]{1,0:T(8,128)(2,1)}), bf16[128,2048]{1,0:T(8,128)(2,1)}) %reduce-scatter.12.cloned.1.call-update) | async-done | bytes 524304 | tf_op jit(solution)/shard_map/reduce_scatter | solution.py:230
  1416.6 48.9 %reduce-scatter.14.cloned.1.call-done = bf16[128,2048]{1,0:T(8,128)(2,1)} async-done(((bf16[1024,2048]{1,0:T(8,128)(2,1)}), bf16[128,2048]{1,0:T(8,128)(2,1)}) %reduce-scatter.14.cloned.1.call-update) | async-done | bytes 524304 | tf_op jit(solution)/shard_map/reduce_scatter | solution.py:230
  1468.1 26.5 %reduce-scatter.26.cloned.1.call-done = bf16[512,256]{1,0:T(8,128)(2,1)} async-done(((bf16[2048,256]{1,0:T(8,128)(2,1)}), bf16[512,256]{1,0:T(8,128)(2,1)}) %reduce-scatter.26.cloned.1.call-update) | async-done | bytes 262160 | tf_op jit(solution)/shard_map/reduce_scatter | solution.py:79
  1496.3 28.7 %reduce-scatter.24.cloned.1.call-done = bf16[512,256]{1,0:T(8,128)(2,1)} async-done(((bf16[2048,256]{1,0:T(8,128)(2,1)}), bf16[512,256]{1,0:T(8,128)(2,1)}) %reduce-scatter.24.cloned.1.call-update) | async-done | bytes 262160 | tf_op jit(solution)/shard_map/reduce_scatter | solution.py:76
  1526.8 29.1 %reduce-scatter.22.cloned.1.call-done = bf16[512,256]{1,0:T(8,128)(2,1)} async-done(((bf16[2048,256]{1,0:T(8,128)(2,1)}), bf16[512,256]{1,0:T(8,128)(2,1)}) %reduce-scatter.22.cloned.1.call-update) | async-done | bytes 262160 | tf_op jit(solution)/shard_map/reduce_scatter | solution.py:73
  1557.7 29.4 %reduce-scatter.20.cloned.1.call-done = bf16[512,256]{1,0:T(8,128)(2,1)} async-done(((bf16[2048,256]{1,0:T(8,128)(2,1)}), bf16[512,256]{1,0:T(8,128)(2,1)}) %reduce-scatter.20.cloned.1.call-update) | async-done | bytes 262160 | tf_op jit(solution)/shard_map/reduce_scatter | solution.py:70
  1589.0 50.6 %reduce-scatter.18.cloned.1.call-done = bf16[128,2048]{1,0:T(8,128)(2,1)} async-done(((bf16[1024,2048]{1,0:T(8,128)(2,1)}), bf16[128,2048]{1,0:T(8,128)(2,1)}) %reduce-scatter.18.cloned.1.call-update) | async-done | bytes 524304 | tf_op jit(solution)/shard_map/reduce_scatter | solution.py:279
  1639.6 50.4 %reduce-scatter.16.cloned.1.call-done = bf16[128,2048]{1,0:T(8,128)(2,1)} async-done(((bf16[1024,2048]{1,0:T(8,128)(2,1)}), bf16[128,2048]{1,0:T(8,128)(2,1)}) %reduce-scatter.16.cloned.1.call-update) | async-done | bytes 524304 | tf_op jit(solution)/shard_map/reduce_scatter | solution.py:279
  1692.0 25.9 %all-reduce.10 = (bf16[2048]{0:T(1024)(128)(2,1)S(1)}, bf16[2048]{0:T(1024)(128)(2,1)S(1)}) all-reduce(f32[2048]{0:T(1024)S(1)} %add.306, f32[2048]{0:T(1024)S(1)} %add.308), channel_id=1, replica_groups=mesh['batch'=4,'head'=8] {'head'}, use_global_device_ids=true, to_apply=%region_37.38 | all-reduce | flops 4096 | bytes 24576 | tf_op jit(solution)/shard_map/psum | solution.py:68
  1718.0 10.0 all-reduce.13
  (447 shorter events, 149.6 us)
Async XLA Ops:
  7.2 17.7 %copy-start.86 = (s32[2,1024]{1,0:T(2,128)S(1)}, s32[2,1024]{1,0:T(2,128)}, u32[]{:S(2)}) copy-start(s32[2,1024]{1,0:T(2,128)} %param.14) | copy-start | bytes 24580
  7.2 17.7 %copy-start.103 = (s32[2,1024]{1,0:T(2,128)S(1)}, s32[2,1024]{1,0:T(2,128)}, u32[]{:S(2)}) copy-start(s32[2,1024]{1,0:T(2,128)} %param.15) | copy-start | bytes 24580
  7.2 32.0 %all-gather.22.cloned.1.call-start = ((), (), s32[]{:S(2)}) async-start(), calls=%async_computation.14 | async-start | bytes 1310720 | tf_op jit(solution)/shard_map/all_gather | solution.py:56
  7.9 80.7 %all-gather.32.cloned.1.call-start = ((), (), s32[]{:S(2)}) async-start(), calls=%async_computation.20 | async-start | bytes 4718592 | tf_op jit(solution)/shard_map/all_gather | solution.py:200
  22.3 93.5 %all-gather.20.cloned.1.call-start = ((), (), s32[]{:S(2)}) async-start(), calls=%async_computation.13 | async-start | bytes 1310720 | tf_op jit(solution)/shard_map/all_gather | solution.py:55
  23.0 121.1 %all-gather.18.cloned.1.call-start = ((), (), s32[]{:S(2)}) async-start(), calls=%async_computation.12 | async-start | bytes 1310720 | tf_op jit(solution)/shard_map/all_gather | solution.py:57
  23.6 169.7 %all-gather.16.cloned.1.call-start = ((), (), s32[]{:S(2)}) async-start(), calls=%async_computation.11 | async-start | bytes 4718592 | tf_op jit(solution)/shard_map/all_gather | solution.py:200
  24.2 196.5 %all-gather.24.cloned.1.call-start = ((), (), s32[]{:S(2)}) async-start(), calls=%async_computation.15 | async-start | bytes 1310720 | tf_op jit(solution)/shard_map/all_gather | solution.py:58
  24.8 543.4 %all-reduce.19.cloned.1.call-start = ((), (), s32[]{:S(2)}) async-start(), calls=%async_computation.34 | async-start | bytes 33554432 | tf_op jit(solution)/shard_map/psum | solution.py:223
  25.9 93.7 %copy-start.68 = (f32[1024,32]{0,1:T(8,128)}, f32[1024,32]{0,1:T(8,128)S(1)}, u32[]{:S(2)}) copy-start(f32[1024,32]{0,1:T(8,128)S(1)} %get-tuple-element.117) | copy-start | bytes 393220
  25.9 93.7 %copy-start.70 = (f32[1024,32]{0,1:T(8,128)}, f32[1024,32]{0,1:T(8,128)S(1)}, u32[]{:S(2)}) copy-start(f32[1024,32]{0,1:T(8,128)S(1)} %get-tuple-element.118) | copy-start | bytes 393220
  25.9 172.3 %copy-start.64 = (f32[1024,32]{0,1:T(8,128)}, f32[1024,32]{0,1:T(8,128)S(1)}, u32[]{:S(2)}) copy-start(f32[1024,32]{0,1:T(8,128)S(1)} %get-tuple-element.109) | copy-start | bytes 393220
  25.9 172.3 %copy-start.66 = (f32[1024,32]{0,1:T(8,128)}, f32[1024,32]{0,1:T(8,128)S(1)}, u32[]{:S(2)}) copy-start(f32[1024,32]{0,1:T(8,128)S(1)} %get-tuple-element.110) | copy-start | bytes 393220
  121.9 26.3 %copy-start.87 = (f32[4,512]{1,0:T(4,128)}, f32[4,512]{1,0:T(4,128)S(1)}, u32[]{:S(2)}) copy-start(f32[4,512]{1,0:T(4,128)S(1)} %get-tuple-element.125) | copy-start | bytes 24580
  127.3 26.4 %copy-start.89 = (f32[4,512]{1,0:T(4,128)}, f32[4,512]{1,0:T(4,128)S(1)}, u32[]{:S(2)}) copy-start(f32[4,512]{1,0:T(4,128)S(1)} %get-tuple-element.123) | copy-start | bytes 24580
  129.6 18.5 %copy-start.91 = (f32[4,512]{1,0:T(4,128)}, f32[4,512]{1,0:T(4,128)S(1)}, u32[]{:S(2)}) copy-start(f32[4,512]{1,0:T(4,128)S(1)} %fusion.2) | copy-start | bytes 24580
  154.4 38.9 %copy-start.19 = (bf16[2048,256]{1,0:T(8,128)(2,1)S(1)}, bf16[2048,256]{1,0:T(8,128)(2,1)}, u32[]{:S(2)}) copy-start(bf16[2048,256]{1,0:T(8,128)(2,1)} %all-gather.22.cloned.1.call-done) | copy-start | bytes 3145732
  168.0 28.9 %copy-start.21 = (bf16[2048,256]{1,0:T(8,128)(2,1)S(1)}, bf16[2048,256]{1,0:T(8,128)(2,1)}, u32[]{:S(2)}) copy-start(bf16[2048,256]{1,0:T(8,128)(2,1)} %all-gather.20.cloned.1.call-done) | copy-start | bytes 3145732
  202.3 7.5 copy-start.4
  202.3 7.5 copy-start.97
  209.9 10.9 copy-start.14
  212.1 14.5 copy-start.16
  234.5 388.4 %all-gather.28.cloned.1.call-start = ((), (), s32[]{:S(2)}) async-start(), calls=%async_computation.17 | async-start | bytes 5242880 | tf_op jit(solution)/shard_map/all_gather | solution.py:60
  235.2 442.3 %all-gather.26.cloned.1.call-start = ((), (), s32[]{:S(2)}) async-start(), calls=%async_computation.16 | async-start | bytes 5242880 | tf_op jit(solution)/shard_map/all_gather | solution.py:59
  236.0 495.9 %all-gather.30.cloned.1.call-start = ((), (), s32[]{:S(2)}) async-start(), calls=%async_computation.18 | async-start | bytes 5242880 | tf_op jit(solution)/shard_map/all_gather | solution.py:61
  236.5 544.7 %all-gather.36.cloned.1.call-start = ((), (), s32[]{:S(2)}) async-start(), calls=%async_computation.32 | async-start | bytes 4718592 | tf_op jit(solution)/shard_map/all_gather | solution.py:235
  237.7 591.5 %all-gather.34.cloned.1.call-start = ((), (), s32[]{:S(2)}) async-start(), calls=%async_computation.31 | async-start | bytes 4718592 | tf_op jit(solution)/shard_map/all_gather | solution.py:235
  238.2 957.6 %all-reduce.17.cloned.1.call-start = ((), (), s32[]{:S(2)}) async-start(), calls=%async_computation.33 | async-start | bytes 33554432 | tf_op jit(solution)/shard_map/psum | solution.py:247
  246.4 328.2 %copy-start.78 = (f32[4,1,512]{2,1,0:T(1,128)}, f32[4,1,512]{2,1,0:T(1,128)S(1)}, u32[]{:S(2)}) copy-start(f32[4,1,512]{2,1,0:T(1,128)S(1)} %convert_element_type.370) | copy-start | bytes 24580
  781.3 13.2 copy-start.117
  829.2 13.2 copy-start.118
  842.4 13.7 copy-start.122
  863.4 498.8 %reduce-scatter.32.cloned.1.call-start = ((), (), s32[]{:S(2)}) async-start(), calls=%async_computation.30 | async-start | bytes 5242880 | tf_op jit(solution)/shard_map/reduce_scatter | solution.py:88
  876.4 488.4 %reduce-scatter.30.cloned.1.call-start = ((), (), s32[]{:S(2)}) async-start(), calls=%async_computation.29 | async-start | bytes 5242880 | tf_op jit(solution)/shard_map/reduce_scatter | solution.py:85
  876.5 7.2 copy-start.25
  889.9 477.7 %reduce-scatter.28.cloned.1.call-start = ((), (), s32[]{:S(2)}) async-start(), calls=%async_computation.28 | async-start | bytes 5242880 | tf_op jit(solution)/shard_map/reduce_scatter | solution.py:82
  890.0 7.4 copy-start.26
  890.0 7.4 copy-start.125
  903.6 511.5 %reduce-scatter.12.cloned.1.call-start = ((), (), s32[]{:S(2)}) async-start(), calls=%async_computation.19 | async-start | bytes 4718592 | tf_op jit(solution)/shard_map/reduce_scatter | solution.py:230
  913.1 552.4 %reduce-scatter.14.cloned.1.call-start = ((), (), s32[]{:S(2)}) async-start(), calls=%async_computation.21 | async-start | bytes 4718592 | tf_op jit(solution)/shard_map/reduce_scatter | solution.py:230
  922.3 273.5 %copy-start.79 = (f32[4,1,512]{2,1,0:T(1,128)S(1)}, f32[4,1,512]{2,1,0:T(1,128)}, u32[]{:S(2)}) copy-start(f32[4,1,512]{2,1,0:T(1,128)} %copy-done.78) | copy-start | bytes 24580
  922.3 273.5 %copy-start.81 = (f32[1024]{0:T(1024)S(1)}, f32[1024]{0:T(1024)}, u32[]{:S(2)}) copy-start(f32[1024]{0:T(1024)} %copy-done.80) | copy-start | bytes 12292
  922.3 273.5 %copy-start.83 = (f32[1024]{0:T(1024)S(1)}, f32[1024]{0:T(1024)}, u32[]{:S(2)}) copy-start(f32[1024]{0:T(1024)} %copy-done.82) | copy-start | bytes 12292
  922.3 572.2 %reduce-scatter.26.cloned.1.call-start = ((), (), s32[]{:S(2)}) async-start(), calls=%async_computation.27 | async-start | bytes 1310720 | tf_op jit(solution)/shard_map/reduce_scatter | solution.py:79
  1210.4 22.6 %copy-start.13 = (bf16[2048,256]{1,0:T(8,128)(2,1)S(1)}, bf16[2048,256]{1,0:T(8,128)(2,1)}, u32[]{:S(2)}) copy-start(bf16[2048,256]{1,0:T(8,128)(2,1)} %all-gather.24.cloned.1.call-done) | copy-start | bytes 3145732
  1233.0 13.2 slice-start.16
  1237.9 9.8 slice-start.2
  1237.9 8.3 slice-start.17
  1237.9 10.1 slice-start.3
  1247.7 8.3 slice-start.8
  1248.0 7.9 slice-start.9
  1260.4 11.8 slice-start.12
  1260.4 11.8 slice-start.13
  1291.8 20.6 %copy-start.55 = (bf16[4,64,1024]{2,1,0:T(8,128)(2,1)}, bf16[4,64,1024]{2,1,0:T(8,128)(2,1)S(1)}, u32[]{:S(2)}) copy-start(bf16[4,64,1024]{2,1,0:T(8,128)(2,1)S(1)} %fusion.79) | copy-start | bytes 1572868
  1303.9 221.2 %reduce-scatter.24.cloned.1.call-start = ((), (), s32[]{:S(2)}) async-start(), calls=%async_computation.26 | async-start | bytes 1310720 | tf_op jit(solution)/shard_map/reduce_scatter | solution.py:76
  1326.7 229.3 %reduce-scatter.22.cloned.1.call-start = ((), (), s32[]{:S(2)}) async-start(), calls=%async_computation.25 | async-start | bytes 1310720 | tf_op jit(solution)/shard_map/reduce_scatter | solution.py:73
  1329.6 7.4 copy-start.28
  1339.5 247.6 %reduce-scatter.20.cloned.1.call-start = ((), (), s32[]{:S(2)}) async-start(), calls=%async_computation.24 | async-start | bytes 1310720 | tf_op jit(solution)/shard_map/reduce_scatter | solution.py:70
  1346.3 293.3 %reduce-scatter.18.cloned.1.call-start = ((), (), s32[]{:S(2)}) async-start(), calls=%async_computation.23 | async-start | bytes 4718592 | tf_op jit(solution)/shard_map/reduce_scatter | solution.py:279
  1352.8 337.3 %reduce-scatter.16.cloned.1.call-start = ((), (), s32[]{:S(2)}) async-start(), calls=%async_computation.22 | async-start | bytes 4718592 | tf_op jit(solution)/shard_map/reduce_scatter | solution.py:279
  1416.6 273.5 %copy-start.11 = (bf16[2,128,2048]{2,1,0:T(8,128)(2,1)S(1)}, bf16[2,128,2048]{2,1,0:T(8,128)(2,1)}, u32[]{:S(2)}) copy-start(bf16[2,128,2048]{2,1,0:T(8,128)(2,1)} %param.13) | copy-start | bytes 3145732
  1416.6 273.5 %copy-start.77 = (f32[4,1,512]{2,1,0:T(1,128)S(1)}, f32[4,1,512]{2,1,0:T(1,128)}, u32[]{:S(2)}) copy-start(f32[4,1,512]{2,1,0:T(1,128)} %copy-done.76) | copy-start | bytes 24580
  1416.6 273.5 %copy-start.105 = (f32[128]{0:T(128)S(1)}, f32[128]{0:T(128)}, u32[]{:S(2)}) copy-start(f32[128]{0:T(128)} %copy-done.104) | copy-start | bytes 1540
  1416.6 273.5 %copy-start.107 = (f32[128]{0:T(128)S(1)}, f32[128]{0:T(128)}, u32[]{:S(2)}) copy-start(f32[128]{0:T(128)} %copy-done.106) | copy-start | bytes 1540
  (105 other events, 321.8 us)
Sparse Core Ops, SparseCore 0:
  9.9 29.3 all-gather.21
  41.4 47.1 all-gather.31
  90.4 25.3 all-gather.19
  117.5 26.6 all-gather.17
  146.2 47.0 all-gather.15
  195.0 25.7 all-gather.23
  234.6 333.5 all-reduce.18
  570.0 52.7 all-gather.27
  624.7 52.6 all-gather.25
  679.2 52.6 all-gather.29
  734.1 47.1 all-gather.35
  783.3 45.8 all-gather.33
  863.5 332.2 all-reduce.16
  1198.6 52.7 reduce-scatter.31
  1254.5 52.6 reduce-scatter.29
  1310.1 52.6 reduce-scatter.27
  1365.0 49.9 reduce-scatter.11
  1417.3 48.1 reduce-scatter.13
  1468.6 25.8 reduce-scatter.25
  1497.3 27.7 reduce-scatter.23
  1528.2 27.7 reduce-scatter.21
  1559.4 27.7 reduce-scatter.19
  1589.6 49.9 reduce-scatter.17
  1641.9 48.1 reduce-scatter.15
where the time goes:
time: 1740 us
  waiting for transfers between devices  1240 us (71%)
  matrix products  291 us (17%)
  other arithmetic  115 us (7%)
  blocking collectives  53.5 us (3%)
  local copies, waits for them, and re-layouts  26.5 us (2%)
    psum x1, waiting for transfers between devices, per_device(): mixed_full = lax.psum(attn_terms + placed, 'head')  322 us
    psum x1, waiting for transfers between devices, per_device(): grad_mlp_in = lax.psum(mlp_in_terms, 'head')  273 us
    reduce_scatter x2, waiting for transfers between devices, per_device(): lax.psum_scatter(attn_in_terms.astype(jnp.bfloat16), 'head', scatter_dime...  101 us
    reduce_scatter x2, waiting for transfers between devices, per_device(): lax.psum_scatter(mlp_terms.astype(jnp.bfloat16), 'head', scatter_dimensio...  93.6 us
    all_gather x2, waiting for transfers between devices, per_device(): lax.all_gather(normed(inputs, gain_one).astype(jnp.bfloat16), 'head', axi...  74.6 us
    dot_general x14, matrix products, contract_cols(): lax.dot_general(left, right, (((1,), (1,)), ((), ())), preferred_element_...  69.3 us
    all_gather x2, waiting for transfers between devices, per_device(): grad_full = lax.all_gather(grad_row, 'head', axis=0, tiled=True)  64.9 us
    dot_general x14, matrix products, contract_rows(): lax.dot_general(left, right, (((0,), (0,)), ((), ())), preferred_element_...  57.6 us
  transfers between devices with their start and end apart: 24, of which 21 were waited for; matrix products, arithmetic and copies ran while one was open for 20% of the time, Pallas kernels for 0%

commit v1 on v0

--- a/solution.py
+++ b/solution.py
@@ -244,7 +244,11 @@
         grad_gate = contract_rows(mlp_in, grad_gate_act)
         grad_up = contract_rows(mlp_in, grad_up_act)
         mlp_in_terms = contract_cols(grad_gate_act, gate_w) + contract_cols(grad_up_act, up_w)
-        grad_mlp_in = lax.psum(mlp_in_terms, "head")
+        grad_mlp_in = mlp_in_terms
+        for hop in (1, 2, 4):
+            grad_mlp_in = grad_mlp_in + lax.ppermute(
+                grad_mlp_in, "head", [(dev, dev ^ hop) for dev in range(8)]
+            )
         grad_from_norm, gain_terms = norm_back(mixed_full, gain_two, grad_mlp_in)
         gain_two_grad = jnp.sum(jnp.where(own_rows[:, None], gain_terms, 0.0), axis=0)
         grad_mixed_full = grad_full.astype(jnp.float32) + grad_from_norm

time: 1740 us -> 2300 us (1.32)
  waiting for transfers between devices: 1240 us -> 1740 us
  other arithmetic: 115 us -> 170 us
    ppermute x0 -> x6, waiting for transfers between devices: none -> 942 us  [per_device(): lax.ppermute(grad_mlp_in, 'head', [(dev, dev ^ hop) for dev in range(8)])]
    psum x1 -> x0, waiting for transfers between devices: 273 us -> none  [per_device(): grad_mlp_in = lax.psum(mlp_in_terms, 'head')]
    reduce_scatter x2, waiting for transfers between devices: 93.6 us -> 0.02 us  [per_device(): lax.psum_scatter(mlp_terms.astype(jnp.bfloat16), 'head', scatter_dimensio...]
    add x0 -> x4, other arithmetic: none -> 48.1 us  [per_device(): grad_mlp_in + lax.ppermute(grad_mlp_in, 'head', [(dev, dev ^ hop) for dev...]
    reduce_scatter x1, waiting for transfers between devices: 28.7 us -> 0.01 us  [reduce_grads(): lax.psum_scatter(grad_parts[2].astype(jnp.bfloat16), 'batch', scatter_dim...]
    reduce_scatter x1, waiting for transfers between devices: 26.5 us -> 0.02 us  [reduce_grads(): lax.psum_scatter(grad_parts[3].astype(jnp.bfloat16), 'batch', scatter_dim...]
  transfers between devices with their start and end apart: 24 -> 29, of which waited for: 21 -> 20; matrix products, arithmetic and copies ran while one was open for 20% -> 18% of each run, Pallas kernels for 0% -> 0%
where the time goes in v1:
time: 2300 us
  waiting for transfers between devices  1740 us (76%)
  matrix products  285 us (12%)
  other arithmetic  170 us (7%)
  blocking collectives  53.4 us (2%)
  local copies, waits for them, and re-layouts  25.6 us (1%)
    ppermute x6, waiting for transfers between devices, per_device(): lax.ppermute(grad_mlp_in, 'head', [(dev, dev ^ hop) for dev in range(8)])  942 us
    psum x1, waiting for transfers between devices, per_device(): mixed_full = lax.psum(attn_terms + placed, 'head')  322 us
    reduce_scatter x2, waiting for transfers between devices, per_device(): lax.psum_scatter(attn_in_terms.astype(jnp.bfloat16), 'head', scatter_dime...  101 us
    all_gather x2, waiting for transfers between devices, per_device(): lax.all_gather(normed(inputs, gain_one).astype(jnp.bfloat16), 'head', axi...  74.6 us
    dot_general x14, matrix products, contract_cols(): lax.dot_general(left, right, (((1,), (1,)), ((), ())), preferred_element_...  67 us
    all_gather x2, waiting for transfers between devices, per_device(): grad_full = lax.all_gather(grad_row, 'head', axis=0, tiled=True)  64.8 us
    dot_general x14, matrix products, contract_rows(): lax.dot_general(left, right, (((0,), (0,)), ((), ())), preferred_element_...  54.4 us
    add x4, other arithmetic, per_device(): grad_mlp_in + lax.ppermute(grad_mlp_in, 'head', [(dev, dev ^ hop) for dev...  48.1 us
  transfers between devices with their start and end apart: 29, of which 20 were waited for; matrix products, arithmetic and copies ran while one was open for 18% of the time, Pallas kernels for 0%

profile of v1, /device:TPU:0, one launch (start us, length us, event | category | flops | bytes accessed | tf_op | source)
XLA Modules:
  0.0 2297.4 jit_solution(13596421283316518290)
XLA Ops:
  8.7 9.5 all-gather.2
  28.9 10.3 all-gather.22.cloned.1.call-done
  39.2 49.3 %all-gather.32.cloned.1.call-done = bf16[1024,2048]{1,0:T(8,128)(2,1)} async-done(((bf16[128,2048]{1,0:T(8,128)(2,1)}), bf16[1024,2048]{1,0:T(8,128)(2,1)}) %all-gather.32.cloned.1.call-update) | async-done | bytes 4194320 | tf_op jit(solution)/shard_map/all_gather | solution.py:200
  92.4 23.4 %all-gather.20.cloned.1.call-done = bf16[2048,256]{1,0:T(8,128)(2,1)} async-done(((bf16[512,256]{1,0:T(8,128)(2,1)}), bf16[2048,256]{1,0:T(8,128)(2,1)}) %all-gather.20.cloned.1.call-update) | async-done | bytes 1048592 | tf_op jit(solution)/shard_map/all_gather | solution.py:55
  121.9 5.4 fusion.142
  129.6 14.5 all-gather.18.cloned.1.call-done
  154.4 13.6 fusion.101
  168.0 25.3 %all-gather.16.cloned.1.call-done = bf16[1024,2048]{1,0:T(8,128)(2,1)} async-done(((bf16[128,2048]{1,0:T(8,128)(2,1)}), bf16[1024,2048]{1,0:T(8,128)(2,1)}) %all-gather.16.cloned.1.call-update) | async-done | bytes 4194320 | tf_op jit(solution)/shard_map/all_gather | solution.py:200
  212.1 8.5 all-gather.24.cloned.1.call-done
  220.6 5.9 fusion.151
  226.4 4.6 fusion.146
  238.1 8.0 all-gather.3
  246.1 321.9 %all-reduce.15.cloned.1.call-done = (f32[1024,2048]{1,0:T(8,128)}, f32[1024,2048]{1,0:T(8,128)}) async-done(((f32[1024,2048]{1,0:T(8,128)}, f32[1024,2048]{1,0:T(8,128)}), (f32[1024,2048]{1,0:T(8,128)}, f32[1024,2048]{1,0:T(8,128)})) %all-reduce.15.cloned.1.call-update) | async-done | bytes 16777232 | tf_op jit(solution)/shard_map/psum | solution.py:223
  576.5 4.5 multiply_convert_fusion.5
  581.0 41.7 %all-gather.28.cloned.1.call-done = bf16[2048,1024]{1,0:T(8,128)(2,1)} async-done(((bf16[512,1024]{1,0:T(8,128)(2,1)}), bf16[2048,1024]{1,0:T(8,128)(2,1)}) %all-gather.28.cloned.1.call-update) | async-done | bytes 4194320 | tf_op jit(solution)/shard_map/all_gather | solution.py:60
  622.7 10.1 fusion.153
  632.8 44.5 %all-gather.26.cloned.1.call-done = bf16[2048,1024]{1,0:T(8,128)(2,1)} async-done(((bf16[512,1024]{1,0:T(8,128)(2,1)}), bf16[2048,1024]{1,0:T(8,128)(2,1)}) %all-gather.26.cloned.1.call-update) | async-done | bytes 4194320 | tf_op jit(solution)/shard_map/all_gather | solution.py:59
  677.3 10.0 fusion.152
  687.3 44.4 %all-gather.30.cloned.1.call-done = bf16[2048,1024]{1,0:T(8,128)(2,1)} async-done(((bf16[512,1024]{1,0:T(8,128)(2,1)}), bf16[2048,1024]{1,0:T(8,128)(2,1)}) %all-gather.30.cloned.1.call-update) | async-done | bytes 4194320 | tf_op jit(solution)/shard_map/all_gather | solution.py:61
  731.8 49.4 %all-gather.36.cloned.1.call-done = bf16[1,1024,2048]{2,1,0:T(8,128)(2,1)} async-done(((bf16[1,128,2048]{2,1,0:T(8,128)(2,1)}), bf16[1,1024,2048]{2,1,0:T(8,128)(2,1)}) %all-gather.36.cloned.1.call-update) | async-done | bytes 4194320 | tf_op jit(solution)/shard_map/all_gather | solution.py:235
  781.1 13.2 multiply_convert_fusion.6
  794.4 7.0 fusion.23
  801.4 6.1 fusion.148
  807.5 6.1 fusion.147
  813.6 15.5 all-gather.34.cloned.1.call-done
  829.1 13.9 multiply_convert_fusion.7
  844.3 8.4 fusion.22
  852.8 7.4 fusion.154
  860.2 6.8 convolution_add_fusion.1
  867.3 4.6 fusion.164
  871.8 6.1 add_convert_fusion.1
  878.1 7.7 fusion.157
  885.8 6.8 convolution_add_fusion
  892.8 4.6 fusion.163
  897.4 6.1 add_convert_fusion.2
  903.8 12.0 add.294
  915.8 12.3 add.307
  930.0 6.1 convolution_convert_fusion.1
  936.2 202.6 %collective-permute-done.1 = f32[1024,2048]{1,0:T(8,128)} collective-permute-done((f32[1024,2048]{1,0:T(8,128)}, f32[1024,2048]{1,0:T(8,128)}, u32[]{:S(2)}, u32[]{:S(2)}) %collective-permute-start.1) | collective-permute-done | bytes 8388640 | tf_op jit(solution)/shard_map/ppermute | solution.py:249
  1138.7 11.8 add.295
  1151.7 331.2 %collective-permute-done.4 = f32[1024,2048]{1,0:T(8,128)} collective-permute-done((f32[1024,2048]{1,0:T(8,128)}, f32[1024,2048]{1,0:T(8,128)}, u32[]{:S(2)}, u32[]{:S(2)}) %collective-permute-start.4) | collective-permute-done | bytes 8388640 | tf_op jit(solution)/shard_map/ppermute | solution.py:249
  1482.9 12.0 add.308
  1495.1 8.4 convolution_convert_fusion
  1503.8 216.3 %collective-permute-done.2 = f32[1024,2048]{1,0:T(8,128)} collective-permute-done((f32[1024,2048]{1,0:T(8,128)}, f32[1024,2048]{1,0:T(8,128)}, u32[]{:S(2)}, u32[]{:S(2)}) %collective-permute-start.2) | collective-permute-done | bytes 8388640 | tf_op jit(solution)/shard_map/ppermute | solution.py:249
  1720.1 191.8 %collective-permute-done.5 = f32[1024,2048]{1,0:T(8,128)} collective-permute-done((f32[1024,2048]{1,0:T(8,128)}, f32[1024,2048]{1,0:T(8,128)}, u32[]{:S(2)}, u32[]{:S(2)}) %collective-permute-start.5) | collective-permute-done | bytes 8388640 | tf_op jit(solution)/shard_map/ppermute | solution.py:249
  1911.8 19.0 select_reduce_fusion.1
  1930.8 26.0 %multiply_add_fusion.1 = (f32[1024,2048]{1,0:T(8,128)}, f32[1024,2048]{1,0:T(8,128)}) fusion(f32[1024,2048]{1,0:T(8,128)} %get-tuple-element.50, bf16[1,1024,2048]{2,1,0:T(8,128)(2,1)} %all-gather.34.cloned.1.call-done, f32[1024]{0:T(1024)S(1)} %broadcast_multiply_fusion.1, f32[2048]{0:T(1024)S(1)} %bitcast.256, f32[1024]{0:T(1024)S(1)} %copy-done.86, ...), kind=kLoop, calls=%fused_computation.21 | loop fusion | flops 33554432 | bytes 75522048 | tf_op jit(solution)/shard_map/add | solution.py:254
  1956.8 4.8 fusion.85
  1961.8 8.2 multiply_reduce_fusion.1
  1971.8 4.5 multiply_convert_fusion.1
  1979.6 4.4 multiply_reduce_fusion
  1984.0 6.3 multiply_convert_fusion
  1990.2 4.7 fusion.93
  1994.9 4.4 multiply_reduce_fusion.4
  1999.4 4.4 multiply_convert_fusion.3
  2018.8 6.5 multiply_reduce_fusion.3
  2025.4 7.1 multiply_convert_fusion.2
  2037.7 5.1 fusion.14
  2099.1 14.1 reduce-scatter.22.cloned.1.call-done
  2115.0 29.5 %reduce-scatter.20.cloned.1.call-done = bf16[512,256]{1,0:T(8,128)(2,1)} async-done(((bf16[2048,256]{1,0:T(8,128)(2,1)}), bf16[512,256]{1,0:T(8,128)(2,1)}) %reduce-scatter.20.cloned.1.call-update) | async-done | bytes 262160 | tf_op jit(solution)/shard_map/reduce_scatter | solution.py:70
  2146.2 50.7 %reduce-scatter.18.cloned.1.call-done = bf16[128,2048]{1,0:T(8,128)(2,1)} async-done(((bf16[1024,2048]{1,0:T(8,128)(2,1)}), bf16[128,2048]{1,0:T(8,128)(2,1)}) %reduce-scatter.18.cloned.1.call-update) | async-done | bytes 524304 | tf_op jit(solution)/shard_map/reduce_scatter | solution.py:283
  2196.8 50.6 %reduce-scatter.16.cloned.1.call-done = bf16[128,2048]{1,0:T(8,128)(2,1)} async-done(((bf16[1024,2048]{1,0:T(8,128)(2,1)}), bf16[128,2048]{1,0:T(8,128)(2,1)}) %reduce-scatter.16.cloned.1.call-update) | async-done | bytes 524304 | tf_op jit(solution)/shard_map/reduce_scatter | solution.py:283
  2249.4 26.0 %all-reduce.10 = (bf16[2048]{0:T(1024)(128)(2,1)S(1)}, bf16[2048]{0:T(1024)(128)(2,1)S(1)}) all-reduce(f32[2048]{0:T(1024)S(1)} %add.326, f32[2048]{0:T(1024)S(1)} %add.328), channel_id=1, replica_groups=mesh['batch'=4,'head'=8] {'head'}, use_global_device_ids=true, to_apply=%region_35.36 | all-reduce | flops 4096 | bytes 24576 | tf_op jit(solution)/shard_map/psum | solution.py:68
  2275.4 10.0 all-reduce.12
  (468 shorter events, 164.6 us)
Async XLA Ops:
  7.2 17.7 copy-start.87
  7.2 17.7 copy-start.106
  7.2 32.0 %all-gather.22.cloned.1.call-start = ((), (), s32[]{:S(2)}) async-start(), calls=%async_computation.14 | async-start | bytes 1310720 | tf_op jit(solution)/shard_map/all_gather | solution.py:56
  7.9 80.7 %all-gather.32.cloned.1.call-start = ((), (), s32[]{:S(2)}) async-start(), calls=%async_computation.20 | async-start | bytes 4718592 | tf_op jit(solution)/shard_map/all_gather | solution.py:200
  22.3 93.5 %all-gather.20.cloned.1.call-start = ((), (), s32[]{:S(2)}) async-start(), calls=%async_computation.13 | async-start | bytes 1310720 | tf_op jit(solution)/shard_map/all_gather | solution.py:55
  23.0 121.1 %all-gather.18.cloned.1.call-start = ((), (), s32[]{:S(2)}) async-start(), calls=%async_computation.12 | async-start | bytes 1310720 | tf_op jit(solution)/shard_map/all_gather | solution.py:57
  23.6 169.7 %all-gather.16.cloned.1.call-start = ((), (), s32[]{:S(2)}) async-start(), calls=%async_computation.11 | async-start | bytes 4718592 | tf_op jit(solution)/shard_map/all_gather | solution.py:200
  24.2 196.4 %all-gather.24.cloned.1.call-start = ((), (), s32[]{:S(2)}) async-start(), calls=%async_computation.15 | async-start | bytes 1310720 | tf_op jit(solution)/shard_map/all_gather | solution.py:58
  24.8 543.3 %all-reduce.15.cloned.1.call-start = ((), (), s32[]{:S(2)}) async-start(), calls=%async_computation.33 | async-start | bytes 33554432 | tf_op jit(solution)/shard_map/psum | solution.py:223
  25.9 93.7 %copy-start.71 = (f32[1024,32]{0,1:T(8,128)}, f32[1024,32]{0,1:T(8,128)S(1)}, u32[]{:S(2)}) copy-start(f32[1024,32]{0,1:T(8,128)S(1)} %get-tuple-element.115) | copy-start | bytes 393220
  25.9 93.7 %copy-start.73 = (f32[1024,32]{0,1:T(8,128)}, f32[1024,32]{0,1:T(8,128)S(1)}, u32[]{:S(2)}) copy-start(f32[1024,32]{0,1:T(8,128)S(1)} %get-tuple-element.116) | copy-start | bytes 393220
  25.9 172.3 %copy-start.67 = (f32[1024,32]{0,1:T(8,128)}, f32[1024,32]{0,1:T(8,128)S(1)}, u32[]{:S(2)}) copy-start(f32[1024,32]{0,1:T(8,128)S(1)} %get-tuple-element.107) | copy-start | bytes 393220
  25.9 172.3 %copy-start.69 = (f32[1024,32]{0,1:T(8,128)}, f32[1024,32]{0,1:T(8,128)S(1)}, u32[]{:S(2)}) copy-start(f32[1024,32]{0,1:T(8,128)S(1)} %get-tuple-element.108) | copy-start | bytes 393220
  121.9 26.3 %copy-start.88 = (f32[4,512]{1,0:T(4,128)}, f32[4,512]{1,0:T(4,128)S(1)}, u32[]{:S(2)}) copy-start(f32[4,512]{1,0:T(4,128)S(1)} %get-tuple-element.123) | copy-start | bytes 24580
  127.3 26.4 %copy-start.90 = (f32[4,512]{1,0:T(4,128)}, f32[4,512]{1,0:T(4,128)S(1)}, u32[]{:S(2)}) copy-start(f32[4,512]{1,0:T(4,128)S(1)} %get-tuple-element.121) | copy-start | bytes 24580
  129.6 18.5 copy-start.92
  154.4 38.9 %copy-start.20 = (bf16[2048,256]{1,0:T(8,128)(2,1)S(1)}, bf16[2048,256]{1,0:T(8,128)(2,1)}, u32[]{:S(2)}) copy-start(bf16[2048,256]{1,0:T(8,128)(2,1)} %all-gather.22.cloned.1.call-done) | copy-start | bytes 3145732
  168.0 28.9 %copy-start.22 = (bf16[2048,256]{1,0:T(8,128)(2,1)S(1)}, bf16[2048,256]{1,0:T(8,128)(2,1)}, u32[]{:S(2)}) copy-start(bf16[2048,256]{1,0:T(8,128)(2,1)} %all-gather.20.cloned.1.call-done) | copy-start | bytes 3145732
  212.1 14.4 copy-start.16
  234.3 388.5 %all-gather.28.cloned.1.call-start = ((), (), s32[]{:S(2)}) async-start(), calls=%async_computation.17 | async-start | bytes 5242880 | tf_op jit(solution)/shard_map/all_gather | solution.py:60
  235.0 442.3 %all-gather.26.cloned.1.call-start = ((), (), s32[]{:S(2)}) async-start(), calls=%async_computation.16 | async-start | bytes 5242880 | tf_op jit(solution)/shard_map/all_gather | solution.py:59
  235.8 496.0 %all-gather.30.cloned.1.call-start = ((), (), s32[]{:S(2)}) async-start(), calls=%async_computation.18 | async-start | bytes 5242880 | tf_op jit(solution)/shard_map/all_gather | solution.py:61
  236.4 544.8 %all-gather.36.cloned.1.call-start = ((), (), s32[]{:S(2)}) async-start(), calls=%async_computation.32 | async-start | bytes 4718592 | tf_op jit(solution)/shard_map/all_gather | solution.py:235
  237.5 591.6 %all-gather.34.cloned.1.call-start = ((), (), s32[]{:S(2)}) async-start(), calls=%async_computation.31 | async-start | bytes 4718592 | tf_op jit(solution)/shard_map/all_gather | solution.py:235
  238.1 1844.8 %reduce-scatter.32.cloned.1.call-start = ((), (), s32[]{:S(2)}) async-start(), calls=%async_computation.30 | async-start | bytes 5242880 | tf_op jit(solution)/shard_map/reduce_scatter | solution.py:88
  246.1 328.3 %copy-start.81 = (f32[4,1,512]{2,1,0:T(1,128)}, f32[4,1,512]{2,1,0:T(1,128)S(1)}, u32[]{:S(2)}) copy-start(f32[4,1,512]{2,1,0:T(1,128)S(1)} %convert_element_type.370) | copy-start | bytes 24580
  781.1 13.2 copy-start.18
  829.1 15.2 copy-start.19
  852.7 1232.7 %reduce-scatter.30.cloned.1.call-start = ((), (), s32[]{:S(2)}) async-start(), calls=%async_computation.29 | async-start | bytes 5242880 | tf_op jit(solution)/shard_map/reduce_scatter | solution.py:85
  867.0 36.8 %collective-permute-start = (f32[1024,2048]{1,0:T(8,128)}, f32[1024,2048]{1,0:T(8,128)}, u32[]{:S(2)}, u32[]{:S(2)}) collective-permute-start(f32[1024,2048]{1,0:T(8,128)} %convolution_add_fusion.1), channel_id=1, source_target_pairs={{0,1},{1,0},{2,3},{3,2},{4,5},{5,4},{6,7},{7,6},{8,9},{9,8},{10,11... | collective-permute-start | bytes 25165832 | tf_op jit(solution)/shard_map/ppermute | solution.py:249
  878.0 1210.3 %reduce-scatter.28.cloned.1.call-start = ((), (), s32[]{:S(2)}) async-start(), calls=%async_computation.28 | async-start | bytes 5242880 | tf_op jit(solution)/shard_map/reduce_scatter | solution.py:82
  892.6 23.2 %collective-permute-start.3 = (f32[1024,2048]{1,0:T(8,128)}, f32[1024,2048]{1,0:T(8,128)}, u32[]{:S(2)}, u32[]{:S(2)}) collective-permute-start(f32[1024,2048]{1,0:T(8,128)} %convolution_add_fusion), channel_id=1, source_target_pairs={{0,1},{1,0},{2,3},{3,2},{4,5},{5,4},{6,7},{7,6},{8,9},{9,8},{10,11... | collective-permute-start | bytes 25165832 | tf_op jit(solution)/shard_map/ppermute | solution.py:249
  903.6 1187.5 %reduce-scatter.12.cloned.1.call-start = ((), (), s32[]{:S(2)}) async-start(), calls=%async_computation.19 | async-start | bytes 4718592 | tf_op jit(solution)/shard_map/reduce_scatter | solution.py:230
  915.8 14.2 copy-start.118
  915.8 14.2 copy-start.128
  915.8 222.9 %collective-permute-start.1 = (f32[1024,2048]{1,0:T(8,128)}, f32[1024,2048]{1,0:T(8,128)}, u32[]{:S(2)}, u32[]{:S(2)}) collective-permute-start(f32[1024,2048]{1,0:T(8,128)} %add.294), channel_id=1, source_target_pairs={{0,2},{1,3},{2,0},{3,1},{4,6},{5,7},{6,4},{7,5},{8,10},{9,11},{10,... | collective-permute-start | bytes 25165832 | tf_op jit(solution)/shard_map/ppermute | solution.py:249
  928.1 554.8 %collective-permute-start.4 = (f32[1024,2048]{1,0:T(8,128)}, f32[1024,2048]{1,0:T(8,128)}, u32[]{:S(2)}, u32[]{:S(2)}) collective-permute-start(f32[1024,2048]{1,0:T(8,128)} %add.307), channel_id=1, source_target_pairs={{0,2},{1,3},{2,0},{3,1},{4,6},{5,7},{6,4},{7,5},{8,10},{9,11},{10,... | collective-permute-start | bytes 25165832 | tf_op jit(solution)/shard_map/ppermute | solution.py:249
  936.1 1156.7 %reduce-scatter.14.cloned.1.call-start = ((), (), s32[]{:S(2)}) async-start(), calls=%async_computation.21 | async-start | bytes 4718592 | tf_op jit(solution)/shard_map/reduce_scatter | solution.py:230
  1150.6 344.3 %copy-start.89 = (f32[4,512]{1,0:T(4,128)S(1)}, f32[4,512]{1,0:T(4,128)}, u32[]{:S(2)}) copy-start(f32[4,512]{1,0:T(4,128)} %copy-done.88) | copy-start | bytes 24580
  1150.6 344.3 %copy-start.93 = (f32[4,512]{1,0:T(4,128)S(1)}, f32[4,512]{1,0:T(4,128)}, u32[]{:S(2)}) copy-start(f32[4,512]{1,0:T(4,128)} %copy-done.92) | copy-start | bytes 24580
  1150.6 344.4 %copy-start.91 = (f32[4,512]{1,0:T(4,128)S(1)}, f32[4,512]{1,0:T(4,128)}, u32[]{:S(2)}) copy-start(f32[4,512]{1,0:T(4,128)} %copy-done.90) | copy-start | bytes 24580
  1150.6 344.4 %copy-start.95 = (f32[4,512]{1,0:T(4,128)S(1)}, f32[4,512]{1,0:T(4,128)}, u32[]{:S(2)}) copy-start(f32[4,512]{1,0:T(4,128)} %copy-done.94) | copy-start | bytes 24580
  1150.6 344.4 %copy-start.97 = (f32[4,512]{1,0:T(4,128)S(1)}, f32[4,512]{1,0:T(4,128)}, u32[]{:S(2)}) copy-start(f32[4,512]{1,0:T(4,128)} %copy-done.96) | copy-start | bytes 24580
  1150.6 344.4 %copy-start.101 = (f32[4,512]{1,0:T(4,128)S(1)}, f32[4,512]{1,0:T(4,128)}, u32[]{:S(2)}) copy-start(f32[4,512]{1,0:T(4,128)} %copy-done.100) | copy-start | bytes 24580
  1150.6 344.4 %copy-start.99 = (f32[4,512]{1,0:T(4,128)S(1)}, f32[4,512]{1,0:T(4,128)}, u32[]{:S(2)}) copy-start(f32[4,512]{1,0:T(4,128)} %copy-done.98) | copy-start | bytes 24580
  1150.6 344.4 %copy-start.103 = (f32[4,512]{1,0:T(4,128)S(1)}, f32[4,512]{1,0:T(4,128)}, u32[]{:S(2)}) copy-start(f32[4,512]{1,0:T(4,128)} %copy-done.102) | copy-start | bytes 24580
  1150.6 344.4 %copy-start.125 = (bf16[1024,1024]{1,0:T(8,128)(2,1)S(1)}, bf16[1024,1024]{1,0:T(8,128)(2,1)}, u32[]{:S(2)}) copy-start(bf16[1024,1024]{1,0:T(8,128)(2,1)} %copy-done.124) | copy-start | bytes 6291460
  1150.6 569.4 %collective-permute-start.2 = (f32[1024,2048]{1,0:T(8,128)}, f32[1024,2048]{1,0:T(8,128)}, u32[]{:S(2)}, u32[]{:S(2)}) collective-permute-start(f32[1024,2048]{1,0:T(8,128)} %add.295), channel_id=1, source_target_pairs={{0,4},{1,5},{2,6},{3,7},{4,0},{5,1},{6,2},{7,3},{8,12},{9,13},{10,... | collective-permute-start | bytes 25165832 | tf_op jit(solution)/shard_map/ppermute | solution.py:249
  1494.9 416.9 %collective-permute-start.5 = (f32[1024,2048]{1,0:T(8,128)}, f32[1024,2048]{1,0:T(8,128)}, u32[]{:S(2)}, u32[]{:S(2)}) collective-permute-start(f32[1024,2048]{1,0:T(8,128)} %add.308), channel_id=1, source_target_pairs={{0,4},{1,5},{2,6},{3,7},{4,0},{5,1},{6,2},{7,3},{8,12},{9,13},{10,... | collective-permute-start | bytes 25165832 | tf_op jit(solution)/shard_map/ppermute | solution.py:249
  1503.5 408.4 %copy-start.82 = (f32[4,1,512]{2,1,0:T(1,128)S(1)}, f32[4,1,512]{2,1,0:T(1,128)}, u32[]{:S(2)}) copy-start(f32[4,1,512]{2,1,0:T(1,128)} %copy-done.81) | copy-start | bytes 24580
  1503.5 408.4 %copy-start.84 = (f32[1024]{0:T(1024)S(1)}, f32[1024]{0:T(1024)}, u32[]{:S(2)}) copy-start(f32[1024]{0:T(1024)} %copy-done.83) | copy-start | bytes 12292
  1503.5 408.4 %copy-start.86 = (f32[1024]{0:T(1024)S(1)}, f32[1024]{0:T(1024)}, u32[]{:S(2)}) copy-start(f32[1024]{0:T(1024)} %copy-done.85) | copy-start | bytes 12292
  1503.5 592.0 %reduce-scatter.26.cloned.1.call-start = ((), (), s32[]{:S(2)}) async-start(), calls=%async_computation.27 | async-start | bytes 1310720 | tf_op jit(solution)/shard_map/reduce_scatter | solution.py:79
  1930.8 26.0 %copy-start.13 = (bf16[2048,256]{1,0:T(8,128)(2,1)S(1)}, bf16[2048,256]{1,0:T(8,128)(2,1)}, u32[]{:S(2)}) copy-start(bf16[2048,256]{1,0:T(8,128)(2,1)} %all-gather.24.cloned.1.call-done) | copy-start | bytes 3145732
  2014.9 19.0 copy-start.58
  2025.3 72.0 %reduce-scatter.24.cloned.1.call-start = ((), (), s32[]{:S(2)}) async-start(), calls=%async_computation.26 | async-start | bytes 1310720 | tf_op jit(solution)/shard_map/reduce_scatter | solution.py:76
  2047.9 65.3 %reduce-scatter.22.cloned.1.call-start = ((), (), s32[]{:S(2)}) async-start(), calls=%async_computation.25 | async-start | bytes 1310720 | tf_op jit(solution)/shard_map/reduce_scatter | solution.py:73
  2060.4 84.0 %reduce-scatter.20.cloned.1.call-start = ((), (), s32[]{:S(2)}) async-start(), calls=%async_computation.24 | async-start | bytes 1310720 | tf_op jit(solution)/shard_map/reduce_scatter | solution.py:70
  2067.2 129.7 %reduce-scatter.18.cloned.1.call-start = ((), (), s32[]{:S(2)}) async-start(), calls=%async_computation.23 | async-start | bytes 4718592 | tf_op jit(solution)/shard_map/reduce_scatter | solution.py:283
  2073.5 174.0 %reduce-scatter.16.cloned.1.call-start = ((), (), s32[]{:S(2)}) async-start(), calls=%async_computation.22 | async-start | bytes 4718592 | tf_op jit(solution)/shard_map/reduce_scatter | solution.py:283
  2092.7 154.7 %copy-start.11 = (bf16[2,128,2048]{2,1,0:T(8,128)(2,1)S(1)}, bf16[2,128,2048]{2,1,0:T(8,128)(2,1)}, u32[]{:S(2)}) copy-start(bf16[2,128,2048]{2,1,0:T(8,128)(2,1)} %param.13) | copy-start | bytes 3145732
  2092.7 154.7 %copy-start.80 = (f32[4,1,512]{2,1,0:T(1,128)S(1)}, f32[4,1,512]{2,1,0:T(1,128)}, u32[]{:S(2)}) copy-start(f32[4,1,512]{2,1,0:T(1,128)} %copy-done.79) | copy-start | bytes 24580
  2092.8 154.7 %copy-start.108 = (f32[128]{0:T(128)S(1)}, f32[128]{0:T(128)}, u32[]{:S(2)}) copy-start(f32[128]{0:T(128)} %copy-done.107) | copy-start | bytes 1540
  2092.8 154.7 %copy-start.110 = (f32[128]{0:T(128)S(1)}, f32[128]{0:T(128)}, u32[]{:S(2)}) copy-start(f32[128]{0:T(128)} %copy-done.109) | copy-start | bytes 1540
  (114 other events, 466.2 us)
Sparse Core Ops, SparseCore 0:
  9.9 29.3 all-gather.21
  41.4 47.1 all-gather.31
  90.4 25.3 all-gather.19
  117.5 26.6 all-gather.17
  146.2 47.0 all-gather.15
  195.0 25.5 all-gather.23
  234.4 333.6 all-reduce.14
  569.9 52.7 all-gather.27
  624.6 52.6 all-gather.25
  679.0 52.6 all-gather.29
  733.9 47.1 all-gather.35
  783.2 45.8 all-gather.33
  852.9 51.3 reduce-scatter.31
  907.4 52.6 reduce-scatter.29
  962.9 52.6 reduce-scatter.27
  1017.9 89.6 reduce-scatter.11
  1503.6 234.9 reduce-scatter.13
  2025.4 26.2 reduce-scatter.25
  2054.7 27.7 reduce-scatter.23
  2085.4 27.7 reduce-scatter.21
  2116.6 27.7 reduce-scatter.19
  2146.8 49.9 reduce-scatter.17
  2199.2 48.1 reduce-scatter.15
